TPU v7x, 32 devices: a whole 2x2x4 slice. The times are simulated.
32 devices in a mesh: row: 4 (over y, x), col: 8 (over z, core).
Axes of the slice: x: 2, y: 2, z: 4, core: 2. Of those that a mesh axis runs over, the one named last changes fastest.
Arguments:
- q_seq: bfloat16 [512, 6144], P('row', 'col'), may hold values from -4.5 to 4.5
- k_seq: bfloat16 [512, 6144], P('row', 'col'), may hold values from -4.5 to 4.5
- v_seq: bfloat16 [512, 6144], P('row', 'col'), may hold values from -6 to 6
- resid: bfloat16 [512, 6144], P('row', 'col'), may hold values from -90 to 90
- ln_gain: float32 [6144], replicated, may hold values from 0.1 to 1.9
- w_up: bfloat16 [6144, 24576], P('row', 'col'), may hold values from -0.078125 to 0.078125
Outputs:
- hidden: bfloat16 [512, 24576], P('row', 'col')
All inputs are finite; a program needn't handle non-finite values.
Results may differ from a plain program's by a relative error of at most 0.0051.
Values may be sent and summed in bfloat16 or wider, within the bound.
A program may use at most 128 MiB of HBM per device.

v0:
```python
import math

import jax
import jax.numpy as jnp
from jax import lax
from jax.sharding import PartitionSpec as P

HD = 128


def attention_block(query, keys, values):
    seq, width = query.shape
    heads = width // HD
    qshaped = query.reshape(seq, heads, HD)
    kshaped = keys.reshape(seq, heads, HD)
    vshaped = values.reshape(seq, heads, HD)
    scores = jnp.einsum("qhd,khd->hqk", qshaped, kshaped, preferred_element_type=jnp.float32)
    scores = scores * (1.0 / math.sqrt(HD))
    rows_idx = lax.broadcasted_iota(jnp.int32, (seq, seq), 0)
    cols_idx = lax.broadcasted_iota(jnp.int32, (seq, seq), 1)
    scores = jnp.where((rows_idx >= cols_idx)[None], scores, -1e30)
    highest = jnp.max(scores, axis=-1, keepdims=True)
    expo = jnp.exp(scores - highest)
    prob = (expo / jnp.sum(expo, axis=-1, keepdims=True)).astype(jnp.bfloat16)
    output = jnp.einsum("hqk,khd->qhd", prob, vshaped, preferred_element_type=jnp.float32)
    return output.astype(jnp.bfloat16).reshape(seq, width)


def scale_rows(stream, mean, spread, gain):
    return ((stream - mean) * lax.rsqrt(spread + 1e-05) * gain[None, :]).astype(jnp.bfloat16)


def per_device(q_seq, k_seq, v_seq, resid, ln_gain, w_up):
    ncols = lax.axis_size("col")
    attended = attention_block(q_seq, k_seq, v_seq)
    stream = resid.astype(jnp.float32) + attended.astype(jnp.float32)
    local_width = stream.shape[1]
    summed, squares = lax.psum((jnp.sum(stream, axis=1), jnp.sum(stream * stream, axis=1)), "col")
    full_width = local_width * ncols
    mean = summed[:, None] / full_width
    spread = squares[:, None] / full_width - mean * mean
    gain_part = lax.dynamic_slice_in_dim(ln_gain, lax.axis_index("col") * local_width, local_width)
    normed = scale_rows(stream, mean, spread, gain_part)
    whole = lax.all_gather(normed, "col", axis=1, tiled=True)
    product = jnp.dot(
        whole, lax.all_gather(w_up, "row", axis=0, tiled=True), preferred_element_type=jnp.float32
    )
    return jax.nn.gelu(product, approximate=True).astype(jnp.bfloat16)


def solution(mesh):
    placed = (
        P("row", "col"),
        P("row", "col"),
        P("row", "col"),
        P("row", "col"),
        P(),
        P("row", "col"),
    )
    return jax.shard_map(
        per_device, mesh=mesh, in_specs=placed, out_specs=P("row", "col"), check_vma=False
    )
```

profile of v0, /device:TPU:0, one launch (start us, length us, event | category | flops | bytes accessed | tf_op | source)
XLA Modules:
  0.0 410.2 jit_solution(15839929872780707893)
XLA Ops:
  6.5 0.0 copy-start.1
  6.5 0.0 all-gather.3.cloned.1.call-start
  6.6 1.1 copy.12
  7.7 1.1 copy.13
  8.8 0.3 fusion.11
  9.1 0.1 fusion.16
  9.2 0.0 copy-done.1
  9.2 0.0 copy-start
  9.2 0.2 copy.16
  9.4 0.3 fusion.12
  9.6 0.2 copy.18
  9.8 0.8 dynamic_slice.3
  10.6 0.0 copy-done
  10.6 0.1 fusion.14
  10.7 18.1 %all-reduce = (f32[128]{0:T(128)S(1)}, f32[128]{0:T(128)S(1)}) all-reduce(f32[128]{0:T(128)S(1)} %get-tuple-element.6, f32[128]{0:T(128)S(1)} %get-tuple-element.5), channel_id=1, replica_groups=mesh['row'=4,'col'=8] {'col'}, use_global_device_ids=true, to_apply=%region_5.6 | all-reduce | flops 256 | bytes 2048 | tf_op jit(solution)/shard_map/psum | solution.py:38
  28.8 0.8 multiply_convert_fusion
  29.6 0.0 all-gather.3.cloned.1.call-update
  29.6 0.0 all-gather.5.cloned.1.call-start
  29.7 0.7 all-gather.5.cloned.1.call-update
  30.4 22.7 %all-gather.3.cloned.1.call-done = bf16[128,6144]{1,0:T(8,128)(2,1)} async-done(((bf16[128,768]{1,0:T(8,128)(2,1)}), bf16[128,6144]{1,0:T(8,128)(2,1)}) %all-gather.3.cloned.1.call-update) | async-done | bytes 1572880 | tf_op jit(solution)/shard_map/all_gather | solution.py:44
  53.1 334.4 %all-gather.5.cloned.1.call-done = bf16[6144,3072]{1,0:T(8,128)(2,1)} async-done(((bf16[1536,3072]{1,0:T(8,128)(2,1)}), bf16[6144,3072]{1,0:T(8,128)(2,1)}) %all-gather.5.cloned.1.call-update) | async-done | bytes 37748752 | tf_op jit(solution)/shard_map/all_gather | solution.py:46
  387.5 15.9 %fusion.8 = bf16[128,3072]{1,0:T(8,128)(2,1)} fusion(bf16[128,6144]{1,0:T(8,128)(2,1)} %all-gather.3.cloned.1.call-done, bf16[6144,3072]{1,0:T(8,128)(2,1)} %all-gather.5.cloned.1.call-done), kind=kOutput, calls=%fused_computation.9 | convolution fusion | flops 4835377152 | bytes 40108032 | tf_op jit(solution)/shard_map/dot_general | solution.py:45
  (2 shorter events, 0.0 us)
Async XLA Ops:
  6.5 2.6 copy-start.1
  6.5 46.5 %all-gather.3.cloned.1.call-start = ((), (), s32[]{:S(2)}) async-start(), calls=%async_computation | async-start | bytes 1769472 | tf_op jit(solution)/shard_map/all_gather | solution.py:44
  9.2 1.4 copy-start
  29.6 357.9 %all-gather.5.cloned.1.call-start = ((), (), s32[]{:S(2)}) async-start(), calls=%async_computation.1 | async-start | bytes 47185920 | tf_op jit(solution)/shard_map/all_gather | solution.py:46
Sparse Core Ops, SparseCore 0:
  29.8 23.2 all-gather.2
  55.0 332.5 all-gather.4
where the time goes:
time: 410 us
  waiting for transfers between devices  358 us (87%)
  blocking collectives  18.1 us (4%)
  matrix products  16.4 us (4%)
  between operations  13.5 us (3%)
    all_gather x1, waiting for transfers between devices, per_device(): lax.all_gather(w_up, 'row', axis=0, tiled=True)  334 us
    all_gather x1, waiting for transfers between devices, per_device(): whole = lax.all_gather(normed, 'col', axis=1, tiled=True)  22.7 us
    psum x1, blocking collectives, per_device(): lax.psum((jnp.sum(stream, axis=1), jnp.sum(stream * stream, axis=1)), 'col')  18.1 us
    dot_general x1, matrix products, per_device(): jnp.dot(whole, lax.all_gather(w_up, 'row', axis=0, tiled=True), preferred...  15.9 us
  transfers between devices with their start and end apart: 2, of which 2 were waited for; matrix products, arithmetic and copies ran while one was open for 0% of the time, Pallas kernels for 0%

commit v1 on v0

v1 whole, which is shorter than its diff:
```python
import functools
import math

import jax
import jax.numpy as jnp
from jax import lax
from jax.experimental import pallas as pl
from jax.experimental.pallas import tpu as pltpu
from jax.sharding import PartitionSpec as P

HD = 128
CORES = 2
CHUNKS = 4
TILE = 512
MESH = pl.DeviceIdType.MESH


def guarded(cond, fn):
    if cond is True:
        fn()
    else:
        pl.when(cond)(fn)


def kernel(
    nrow, ncol,
    q_ref, k_ref, v_ref, resid_ref, gain_ref, w_hbm, out_ref,
    w_ref, stream, stats, zbuf, xbuf, pbuf, rbuf, own, acc_ref,
    w_sem, st_s, st_r, z_s, z_r, p_s, p_r, b_s, b_r, r_s, r_r,
):
    seq, width = q_ref.shape
    cols = out_ref.shape[1]
    ratio = ncol // nrow
    nz = ncol // CORES
    ct = seq // CHUNKS
    full = width * ncol
    row, col = lax.axis_index("row"), lax.axis_index("col")
    z, core = lax.div(col, CORES), lax.rem(col, CORES)
    sibling = z * CORES + 1 - core
    sends = []

    def remote(src, dst, send_sem, recv_sem, dev):
        return pltpu.make_async_remote_copy(
            src_ref=src, dst_ref=dst, send_sem=send_sem, recv_sem=recv_sem,
            device_id=dev, device_id_type=MESH,
        )

    w_copy = pltpu.make_async_copy(w_hbm, w_ref, w_sem)
    w_copy.start()

    barrier = pltpu.get_barrier_semaphore()
    for d in range(1, ncol):
        pl.semaphore_signal(barrier, inc=1, device_id=(row, lax.rem(col + d, ncol)), device_id_type=MESH)
    for d in range(1, nrow):
        pl.semaphore_signal(barrier, inc=1, device_id=(lax.rem(row + d, nrow), col), device_id_type=MESH)

    causal = lax.broadcasted_iota(jnp.int32, (seq, seq), 0) >= lax.broadcasted_iota(jnp.int32, (seq, seq), 1)
    s1 = jnp.zeros((seq, 1), jnp.float32)
    s2 = jnp.zeros((seq, 1), jnp.float32)
    for h in range(width // HD):
        cut = slice(h * HD, (h + 1) * HD)
        scores = lax.dot_general(
            q_ref[:, cut], k_ref[:, cut], (((1,), (1,)), ((), ())), preferred_element_type=jnp.float32
        ) * (1.0 / math.sqrt(HD))
        scores = jnp.where(causal, scores, -1e30)
        expo = jnp.exp(scores - jnp.max(scores, axis=-1, keepdims=True))
        prob = (expo / jnp.sum(expo, axis=-1, keepdims=True)).astype(jnp.bfloat16)
        attended = jnp.dot(prob, v_ref[:, cut], preferred_element_type=jnp.float32).astype(jnp.bfloat16)
        part = resid_ref[:, cut].astype(jnp.float32) + attended.astype(jnp.float32)
        stream[:, cut] = part
        s1 += jnp.sum(part, axis=1, keepdims=True)
        s2 += jnp.sum(part * part, axis=1, keepdims=True)

    lane = lax.broadcasted_iota(jnp.int32, (seq, HD), 1)
    packed = jnp.where(lane == 0, s1, jnp.where(lane == 1, s2, 0.0))
    stats[col] = packed.T[:8]
    pl.semaphore_wait(barrier, ncol + nrow - 2)
    for d in range(1, ncol):
        copy = remote(stats.at[col], stats.at[col], st_s.at[d - 1], st_r.at[col], (row, lax.rem(col + d, ncol)))
        copy.start()
        sends.append((True, copy))
    for d in range(1, ncol):
        other = lax.rem(col + d, ncol)
        remote(stats.at[other], stats.at[other], st_s.at[d - 1], st_r.at[other], (row, other)).wait_recv()
    total = stats[0]
    for c in range(1, ncol):
        total += stats[c]
    spread_out = jnp.concatenate([total] * (seq // 8), axis=0).T
    mean = spread_out[:, 0:1] / full
    spread = spread_out[:, 1:2] / full - mean * mean
    inv = lax.rsqrt(spread + 1e-05)
    gain = gain_ref[:, pl.ds(pl.multiple_of(col * width, 128), width)]

    for s in range(CHUNKS):
        rows = slice(s * ct, (s + 1) * ct)
        zbuf[s, z] = ((stream[rows, :] - mean[rows]) * inv[rows] * gain).astype(jnp.bfloat16)
        for d in range(1, nz):
            dev = (row, lax.rem(z + d, nz) * CORES + core)
            copy = remote(zbuf.at[s, z], zbuf.at[s, z], z_s.at[s, d - 1], z_r.at[s, z], dev)
            copy.start()
            sends.append((True, copy))

    if ratio % CORES == 0:
        mine = [CORES * i + core for i in range(ratio // CORES)]
        theirs = [CORES * i + 1 - core for i in range(ratio // CORES)]
        holds = lambda r: True
        lacks = lambda r: True
    else:
        mine, theirs = [0], [0]
        holds = lambda r: lax.rem(r, CORES) == core
        lacks = lambda r: lax.rem(r, CORES) != core

    def to_rows(s):
        for d in range(1, nz):
            other = lax.rem(z + d, nz)
            remote(
                zbuf.at[s, other], zbuf.at[s, other], z_s.at[s, d - 1], z_r.at[s, other],
                (row, other * CORES + core),
            ).wait_recv()
        for i, j in enumerate(mine):
            for d in range(1, nrow):
                to = lax.rem(row + d, nrow)
                copy = remote(
                    zbuf.at[s, lax.div(to * ratio + j, CORES)], xbuf.at[s, j, row],
                    p_s.at[s, i, d - 1], p_r.at[s, i, row], (to, col),
                )
                guarded(holds(to), copy.start)
                sends.append((holds(to), copy))

            def keep(j=j):
                xbuf[s, j, row] = zbuf[s, lax.div(row * ratio + j, CORES)]

            guarded(holds(row), keep)

    def to_sibling(s):
        for i, j in enumerate(mine):

            def pass_on(i=i, j=j):
                for d in range(1, nrow):
                    src = lax.rem(row + d, nrow)
                    remote(
                        xbuf.at[s, j, src], xbuf.at[s, j, src], p_s.at[s, i, d - 1], p_r.at[s, i, src],
                        (src, col),
                    ).wait_recv()
                remote(xbuf.at[s, j], xbuf.at[s, j], b_s.at[s, i], b_r.at[s, i], (row, sibling)).start()

            guarded(holds(row), pass_on)
            sends.append((
                holds(row),
                remote(xbuf.at[s, j], xbuf.at[s, j], b_s.at[s, i], b_r.at[s, i], (row, sibling)),
            ))

    def multiply(s):
        for i, j in enumerate(theirs):
            copy = remote(xbuf.at[s, j], xbuf.at[s, j], b_s.at[s, i], b_r.at[s, i], (row, sibling))
            guarded(lacks(row), copy.wait_recv)
        if s == 0:
            w_copy.wait()

        @pl.loop(0, cols // TILE)
        def _(n):
            at = pl.ds(pl.multiple_of(n * TILE, TILE), TILE)
            acc = None
            for j in range(ratio):
                term = jnp.dot(
                    xbuf[s, j].reshape(nrow * ct, width), w_ref[j * width:(j + 1) * width, at],
                    preferred_element_type=jnp.float32,
                )
                acc = term if acc is None else acc + term
            acc = acc.reshape(nrow, ct, TILE)
            acc_ref[...] = acc
            pbuf[s, :, :, at] = acc.astype(jnp.bfloat16)
            own[s, :, at] = acc_ref[row]

        for d in range(1, nrow):
            to = lax.rem(row + d, nrow)
            copy = remote(pbuf.at[s, to], rbuf.at[s, row], r_s.at[s, d - 1], r_r.at[s, row], (to, col))
            copy.start()
            sends.append((True, copy))

    def finish(s):
        for d in range(1, nrow):
            src = lax.rem(row + d, nrow)
            remote(
                pbuf.at[s, src], rbuf.at[s, src], r_s.at[s, d - 1], r_r.at[s, src], (src, col)
            ).wait_recv()

        @pl.loop(0, cols // TILE)
        def _(n):
            at = pl.ds(pl.multiple_of(n * TILE, TILE), TILE)
            u = own[s, :, at]
            for d in range(1, nrow):
                u = u + rbuf[s, lax.rem(row + d, nrow), :, at].astype(jnp.float32)
            u = 0.5 * u * (1.0 + jnp.tanh(math.sqrt(2.0 / math.pi) * (u + 0.044715 * (u * u * u))))
            out_ref[s * ct:(s + 1) * ct, at] = u.astype(jnp.bfloat16)

    to_rows(0)
    to_sibling(0)
    for s in range(CHUNKS):
        if s + 1 < CHUNKS:
            to_rows(s + 1)
        multiply(s)
        if s + 1 < CHUNKS:
            to_sibling(s + 1)
    for s in range(CHUNKS):
        finish(s)
    for cond, copy in sends:
        guarded(cond, copy.wait_send)


def per_device(q_seq, k_seq, v_seq, resid, ln_gain, w_up):
    nrow, ncol = lax.axis_size("row"), lax.axis_size("col")
    seq, width = q_seq.shape
    depth, cols = w_up.shape
    ratio, nz, ct = ncol // nrow, ncol // CORES, seq // CHUNKS
    per = max(1, ratio // CORES)
    dma = pltpu.SemaphoreType.DMA
    vmem = pl.BlockSpec(memory_space=pltpu.VMEM)
    return pl.pallas_call(
        functools.partial(kernel, nrow, ncol),
        out_shape=jax.ShapeDtypeStruct((seq, cols), jnp.bfloat16),
        in_specs=[vmem] * 5 + [pl.BlockSpec(memory_space=pl.ANY)],
        out_specs=vmem,
        scratch_shapes=[
            pltpu.VMEM((depth, cols), jnp.bfloat16),
            pltpu.VMEM((seq, width), jnp.float32),
            pltpu.VMEM((ncol, 8, seq), jnp.float32),
            pltpu.VMEM((CHUNKS, nz, ct, width), jnp.bfloat16),
            pltpu.VMEM((CHUNKS, ratio, nrow, ct, width), jnp.bfloat16),
            pltpu.VMEM((CHUNKS, nrow, ct, cols), jnp.bfloat16),
            pltpu.VMEM((CHUNKS, nrow, ct, cols), jnp.bfloat16),
            pltpu.VMEM((CHUNKS, ct, cols), jnp.float32),
            pltpu.VMEM((nrow, ct, TILE), jnp.float32),
            dma,
            dma((ncol - 1,)),
            dma((ncol,)),
            dma((CHUNKS, nz - 1)),
            dma((CHUNKS, nz)),
            dma((CHUNKS, per, nrow - 1)),
            dma((CHUNKS, per, nrow)),
            dma((CHUNKS, per)),
            dma((CHUNKS, per)),
            dma((CHUNKS, nrow - 1)),
            dma((CHUNKS, nrow)),
        ],
        compiler_params=pltpu.CompilerParams(
            collective_id=0, has_side_effects=True, vmem_limit_bytes=48 * 1024 * 1024
        ),
        cost_estimate=pl.CostEstimate(
            flops=2 * nrow * seq * depth * cols,
            bytes_accessed=2 * (depth * cols + seq * cols + 4 * seq * width),
            transcendentals=seq * cols,
        ),
    )(q_seq, k_seq, v_seq, resid, ln_gain.reshape(1, -1), w_up)


def solution(mesh):
    placed = (
        P("row", "col"),
        P("row", "col"),
        P("row", "col"),
        P("row", "col"),
        P(),
        P("row", "col"),
    )
    return jax.shard_map(
        per_device, mesh=mesh, in_specs=placed, out_specs=P("row", "col"), check_vma=False
    )
```

time: 410 us -> 70.9 us (0.17)
  waiting for transfers between devices: 358 us -> 0 us
  Pallas kernels: 0 us -> 64.6 us
  blocking collectives: 18.1 us -> 0 us
  matrix products: 16.4 us -> 0 us
  between operations: 13.5 us -> 0.01 us
    all_gather x2 -> x0, waiting for transfers between devices: 357 us -> none  [the longest x1 334 us: per_device(): lax.all_gather(w_up, 'row', axis=0, tiled=True)]
    pallas_call x0 -> x1, Pallas kernels: none -> 64.6 us  [per_device(): pl.pallas_call(functools.partial(kernel, nrow, ncol), out_shape=jax.Shape...]
    psum x1 -> x0, blocking collectives: 18.1 us -> none  [per_device(): lax.psum((jnp.sum(stream, axis=1), jnp.sum(stream * stream, axis=1)), 'col')]
    dot_general x3 -> x0, matrix products: 16.4 us -> none  [the longest x1 15.9 us: per_device(): jnp.dot(whole, lax.all_gather(w_up, 'row', axis=0, tiled=True), preferred...]
  transfers between devices with their start and end apart: 2 -> 0, of which waited for: 2 -> 0; matrix products, arithmetic and copies ran while one was open for 0% -> 0% of each run, Pallas kernels for 0% -> 0%
where the time goes in v1:
time: 70.9 us; the launch traced here: 69.9 us
  Pallas kernels  64.6 us (91%)
  local copies, waits for them, and re-layouts  5.32 us (8%)
    pallas_call x1, Pallas kernels, per_device(): pl.pallas_call(functools.partial(kernel, nrow, ncol), out_shape=jax.Shape...  64.6 us
    unnamed x11, local copies, waits for them, and re-layouts  5.32 us

profile of v1, /device:TPU:0, one launch (start us, length us, event | category | flops | bytes accessed | tf_op | source)
XLA Modules:
  0.0 69.9 jit_solution(2504057475290334995)
XLA Ops:
  0.0 0.0 copy-start
  0.0 0.9 %copy-done = bf16[128,768]{1,0:T(8,128)(2,1)S(1)} copy-done((bf16[128,768]{1,0:T(8,128)(2,1)S(1)}, bf16[128,768]{1,0:T(8,128)(2,1)}, u32[]{:S(2)}) %copy-start) | copy-done | bytes 196632
  0.9 0.0 copy-start.1
  0.9 0.9 %copy-done.1 = bf16[128,768]{1,0:T(8,128)(2,1)S(1)} copy-done((bf16[128,768]{1,0:T(8,128)(2,1)S(1)}, bf16[128,768]{1,0:T(8,128)(2,1)}, u32[]{:S(2)}) %copy-start.1) | copy-done | bytes 196632
  1.9 0.0 copy-start.2
  1.9 0.9 %copy-done.2 = bf16[128,768]{1,0:T(8,128)(2,1)S(1)} copy-done((bf16[128,768]{1,0:T(8,128)(2,1)S(1)}, bf16[128,768]{1,0:T(8,128)(2,1)}, u32[]{:S(2)}) %copy-start.2) | copy-done | bytes 196632
  2.8 0.0 copy-start.3
  2.8 0.9 %copy-done.3 = bf16[128,768]{1,0:T(8,128)(2,1)S(1)} copy-done((bf16[128,768]{1,0:T(8,128)(2,1)S(1)}, bf16[128,768]{1,0:T(8,128)(2,1)}, u32[]{:S(2)}) %copy-start.3) | copy-done | bytes 196632
  3.7 0.0 copy-start.4
  3.7 0.7 %copy-done.4 = f32[6144]{0:T(1024)S(1)} copy-done((f32[6144]{0:T(1024)S(1)}, f32[6144]{0:T(1024)}, u32[]{:S(2)}) %copy-start.4) | copy-done | bytes 24600
  4.4 64.6 %shard_map.64 = bf16[128,3072]{1,0:T(8,128)(2,1)S(1)} custom-call(bf16[128,768]{1,0:T(8,128)(2,1)S(1)} %copy-done, bf16[128,768]{1,0:T(8,128)(2,1)S(1)} %copy-done.1, bf16[128,768]{1,0:T(8,128)(2,1)S(1)} %copy-done.2, bf16[128,768]{1,0:T(8,128)(2,1)S(1)} %copy-done.3, f32[1,6144]{1,0:T(1,128)S(1)} %bitcast.1, bf16[1536,3072]{1,0:T(8,128)(2,1)} %w_hbm.1), custom_call_target="tpu_custom_call" | custom-call | flops 4831838208 | bytes 11010048 | tf_op jit(solution)/shard_map/pallas_call | solution.py:219
  69.0 0.9 %copy.8 = bf16[128,3072]{1,0:T(8,128)(2,1)} copy(bf16[128,3072]{1,0:T(8,128)(2,1)S(1)} %shard_map.64) | data formatting | bytes 1572864
Async XLA Ops:
  0.0 0.9 %copy-start = (bf16[128,768]{1,0:T(8,128)(2,1)S(1)}, bf16[128,768]{1,0:T(8,128)(2,1)}, u32[]{:S(2)}) copy-start(bf16[128,768]{1,0:T(8,128)(2,1)} %q_ref.1) | copy-start | bytes 589828
  0.9 0.9 %copy-start.1 = (bf16[128,768]{1,0:T(8,128)(2,1)S(1)}, bf16[128,768]{1,0:T(8,128)(2,1)}, u32[]{:S(2)}) copy-start(bf16[128,768]{1,0:T(8,128)(2,1)} %k_ref.1) | copy-start | bytes 589828
  1.9 0.9 %copy-start.2 = (bf16[128,768]{1,0:T(8,128)(2,1)S(1)}, bf16[128,768]{1,0:T(8,128)(2,1)}, u32[]{:S(2)}) copy-start(bf16[128,768]{1,0:T(8,128)(2,1)} %v_ref.1) | copy-start | bytes 589828
  2.8 0.9 %copy-start.3 = (bf16[128,768]{1,0:T(8,128)(2,1)S(1)}, bf16[128,768]{1,0:T(8,128)(2,1)}, u32[]{:S(2)}) copy-start(bf16[128,768]{1,0:T(8,128)(2,1)} %resid_ref.1) | copy-start | bytes 589828
  3.7 0.7 %copy-start.4 = (f32[6144]{0:T(1024)S(1)}, f32[6144]{0:T(1024)}, u32[]{:S(2)}) copy-start(f32[6144]{0:T(1024)} %param.10) | copy-start | bytes 73732

commit v2 on v1

--- a/solution.py
+++ b/solution.py
@@ -22,14 +22,23 @@
         pl.when(cond)(fn)
 
 
+def low_count(nrow):
+    return max(n for n in range(1, math.isqrt(nrow) + 1) if nrow % n == 0)
+
+
 def kernel(
     nrow, ncol,
-    q_ref, k_ref, v_ref, resid_ref, gain_ref, w_hbm, out_ref,
-    w_ref, stream, stats, zbuf, xbuf, pbuf, rbuf, own, acc_ref,
-    w_sem, st_s, st_r, z_s, z_r, p_s, p_r, b_s, b_r, r_s, r_r,
+    q_hbm, k_hbm, v_hbm, resid_hbm, gain_hbm, w_hbm, out_ref,
+    q_ref, k_ref, v_ref, resid_ref, gain_ref, w_ref, stream, stats, zbuf, xbuf, acc_ref,
+    one_p, one_r, one_own, two_p, two_r, two_own, other_one_p, other_one_r, other_one_own,
+    other_two_p, other_two_r, other_two_own,
+    in_sem, w_sem, st_s, st_r, z_s, z_r, p_s, p_r, b_s, b_r,
+    r1_s, r1_r, r2_s, r2_r, q1_s, q1_r, q2_s, q2_r,
 ):
     seq, width = q_ref.shape
     cols = out_ref.shape[1]
+    half = cols // 2
+    tile = math.gcd(half, TILE)
     ratio = ncol // nrow
     nz = ncol // CORES
     ct = seq // CHUNKS
@@ -45,7 +54,16 @@
             device_id=dev, device_id_type=MESH,
         )
 
+    loads = [
+        pltpu.make_async_copy(src, dst, in_sem.at[i])
+        for i, (src, dst) in enumerate((
+            (q_hbm, q_ref), (k_hbm, k_ref), (v_hbm, v_ref), (resid_hbm, resid_ref),
+            (gain_hbm.at[:, pl.ds(pl.multiple_of(col * width, 128), width)], gain_ref),
+        ))
+    ]
     w_copy = pltpu.make_async_copy(w_hbm, w_ref, w_sem)
+    for load in loads:
+        load.start()
     w_copy.start()
 
     barrier = pltpu.get_barrier_semaphore()
@@ -53,6 +71,9 @@
         pl.semaphore_signal(barrier, inc=1, device_id=(row, lax.rem(col + d, ncol)), device_id_type=MESH)
     for d in range(1, nrow):
         pl.semaphore_signal(barrier, inc=1, device_id=(lax.rem(row + d, nrow), col), device_id_type=MESH)
+
+    for load in loads:
+        load.wait()
 
     causal = lax.broadcasted_iota(jnp.int32, (seq, seq), 0) >= lax.broadcasted_iota(jnp.int32, (seq, seq), 1)
     s1 = jnp.zeros((seq, 1), jnp.float32)
@@ -89,7 +110,7 @@
     mean = spread_out[:, 0:1] / full
     spread = spread_out[:, 1:2] / full - mean * mean
     inv = lax.rsqrt(spread + 1e-05)
-    gain = gain_ref[:, pl.ds(pl.multiple_of(col * width, 128), width)]
+    gain = gain_ref[...]
 
     for s in range(CHUNKS):
         rows = slice(s * ct, (s + 1) * ct)
@@ -109,6 +130,22 @@
         mine, theirs = [0], [0]
         holds = lambda r: lax.rem(r, CORES) == core
         lacks = lambda r: lax.rem(r, CORES) != core
+
+    nlow = low_count(nrow)
+    nhigh = nrow // nlow
+    high, low_at = lax.div(row, nlow), lax.rem(row, nlow)
+    ways = [
+        dict(
+            start=0, n1=nlow, n2=nhigh, one=low_at, two=high, index=lambda i, m: m * nlow + i,
+            p1=one_p, r1=one_r, own1=one_own, p2=two_p, r2=two_r, own2=two_own,
+            s1_s=r1_s, s1_r=r1_r, s2_s=r2_s, s2_r=r2_r,
+        ),
+        dict(
+            start=half, n1=nhigh, n2=nlow, one=high, two=low_at, index=lambda i, m: i * nlow + m,
+            p1=other_one_p, r1=other_one_r, own1=other_one_own, p2=other_two_p, r2=other_two_r,
+            own2=other_two_own, s1_s=q1_s, s1_r=q1_r, s2_s=q2_s, s2_r=q2_r,
+        ),
+    ]
 
     def to_rows(s):
         for d in range(1, nz):
@@ -157,42 +194,88 @@
         if s == 0:
             w_copy.wait()
 
-        @pl.loop(0, cols // TILE)
-        def _(n):
-            at = pl.ds(pl.multiple_of(n * TILE, TILE), TILE)
-            acc = None
-            for j in range(ratio):
-                term = jnp.dot(
-                    xbuf[s, j].reshape(nrow * ct, width), w_ref[j * width:(j + 1) * width, at],
-                    preferred_element_type=jnp.float32,
+        for way in ways:
+            start, one, p, kept = way["start"], way["one"], way["p1"], way["own1"]
+
+            @pl.loop(0, half // tile)
+            def _(n):
+                at = pl.ds(pl.multiple_of(n * tile, tile), tile)
+                w_at = pl.ds(pl.multiple_of(start + n * tile, tile), tile)
+                acc = None
+                for j in range(ratio):
+                    term = jnp.dot(
+                        xbuf[s, j].reshape(nrow * ct, width), w_ref[j * width:(j + 1) * width, w_at],
+                        preferred_element_type=jnp.float32,
+                    )
+                    acc = term if acc is None else acc + term
+                acc = acc.reshape(nrow, ct, tile)
+                acc_ref[...] = acc
+                low = acc.astype(jnp.bfloat16)
+                for i in range(way["n1"]):
+                    for m in range(way["n2"]):
+                        p[s, i, m, :, at] = low[way["index"](i, m)]
+                for m in range(way["n2"]):
+                    kept[s, m, :, at] = acc_ref[way["index"](one, m)]
+
+            for d in range(1, way["n1"]):
+                to = lax.rem(one + d, way["n1"])
+                copy = remote(
+                    p.at[s, to], way["r1"].at[s, one], way["s1_s"].at[s, d - 1], way["s1_r"].at[s, one],
+                    (way["index"](to, way["two"]), col),
                 )
-                acc = term if acc is None else acc + term
-            acc = acc.reshape(nrow, ct, TILE)
-            acc_ref[...] = acc
-            pbuf[s, :, :, at] = acc.astype(jnp.bfloat16)
-            own[s, :, at] = acc_ref[row]
-
-        for d in range(1, nrow):
-            to = lax.rem(row + d, nrow)
-            copy = remote(pbuf.at[s, to], rbuf.at[s, row], r_s.at[s, d - 1], r_r.at[s, row], (to, col))
-            copy.start()
-            sends.append((True, copy))
+                copy.start()
+                sends.append((True, copy))
+
+    def add_first(s):
+        for way in ways:
+            one, two = way["one"], way["two"]
+            for d in range(1, way["n1"]):
+                src = lax.rem(one + d, way["n1"])
+                remote(
+                    way["p1"].at[s, src], way["r1"].at[s, src], way["s1_s"].at[s, d - 1], way["s1_r"].at[s, src],
+                    (way["index"](src, two), col),
+                ).wait_recv()
+            for e in list(range(1, way["n2"])) + [0]:
+                to = lax.rem(two + e, way["n2"])
+
+                @pl.loop(0, half // tile)
+                def _(n):
+                    at = pl.ds(pl.multiple_of(n * tile, tile), tile)
+                    u = way["own1"][s, to, :, at]
+                    for d in range(1, way["n1"]):
+                        u = u + way["r1"][s, lax.rem(one + d, way["n1"]), to, :, at].astype(jnp.float32)
+                    if e:
+                        way["p2"][s, to, :, at] = u.astype(jnp.bfloat16)
+                    else:
+                        way["own2"][s, :, at] = u
+
+                if e:
+                    copy = remote(
+                        way["p2"].at[s, to], way["r2"].at[s, two], way["s2_s"].at[s, e - 1],
+                        way["s2_r"].at[s, two], (way["index"](one, to), col),
+                    )
+                    copy.start()
+                    sends.append((True, copy))
 
     def finish(s):
-        for d in range(1, nrow):
-            src = lax.rem(row + d, nrow)
-            remote(
-                pbuf.at[s, src], rbuf.at[s, src], r_s.at[s, d - 1], r_r.at[s, src], (src, col)
-            ).wait_recv()
-
-        @pl.loop(0, cols // TILE)
-        def _(n):
-            at = pl.ds(pl.multiple_of(n * TILE, TILE), TILE)
-            u = own[s, :, at]
-            for d in range(1, nrow):
-                u = u + rbuf[s, lax.rem(row + d, nrow), :, at].astype(jnp.float32)
-            u = 0.5 * u * (1.0 + jnp.tanh(math.sqrt(2.0 / math.pi) * (u + 0.044715 * (u * u * u))))
-            out_ref[s * ct:(s + 1) * ct, at] = u.astype(jnp.bfloat16)
+        for way in ways:
+            one, two = way["one"], way["two"]
+            for e in range(1, way["n2"]):
+                src = lax.rem(two + e, way["n2"])
+                remote(
+                    way["p2"].at[s, src], way["r2"].at[s, src], way["s2_s"].at[s, e - 1],
+                    way["s2_r"].at[s, src], (way["index"](one, src), col),
+                ).wait_recv()
+
+            @pl.loop(0, half // tile)
+            def _(n):
+                at = pl.ds(pl.multiple_of(n * tile, tile), tile)
+                u = way["own2"][s, :, at]
+                for e in range(1, way["n2"]):
+                    u = u + way["r2"][s, lax.rem(two + e, way["n2"]), :, at].astype(jnp.float32)
+                u = 0.5 * u * (1.0 + jnp.tanh(math.sqrt(2.0 / math.pi) * (u + 0.044715 * (u * u * u))))
+                w_at = pl.ds(pl.multiple_of(way["start"] + n * tile, tile), tile)
+                out_ref[s * ct:(s + 1) * ct, w_at] = u.astype(jnp.bfloat16)
 
     to_rows(0)
     to_sibling(0)
@@ -202,7 +285,12 @@
         multiply(s)
         if s + 1 < CHUNKS:
             to_sibling(s + 1)
-    for s in range(CHUNKS):
+        if s:
+            add_first(s - 1)
+    for s in range(CHUNKS - 2):
+        finish(s)
+    add_first(CHUNKS - 1)
+    for s in range(max(CHUNKS - 2, 0), CHUNKS):
         finish(s)
     for cond, copy in sends:
         guarded(cond, copy.wait_send)
@@ -216,21 +304,38 @@
     per = max(1, ratio // CORES)
     dma = pltpu.SemaphoreType.DMA
     vmem = pl.BlockSpec(memory_space=pltpu.VMEM)
+    half = cols // 2
+    tile = math.gcd(half, TILE)
+    nlow = low_count(nrow)
+    nhigh = nrow // nlow
+
+    def sums(n1, n2):
+        return [
+            pltpu.VMEM((CHUNKS, n1, n2, ct, half), jnp.bfloat16),
+            pltpu.VMEM((CHUNKS, n1, n2, ct, half), jnp.bfloat16),
+            pltpu.VMEM((CHUNKS, n2, ct, half), jnp.float32),
+            pltpu.VMEM((CHUNKS, n2, ct, half), jnp.bfloat16),
+            pltpu.VMEM((CHUNKS, n2, ct, half), jnp.bfloat16),
+            pltpu.VMEM((CHUNKS, ct, half), jnp.float32),
+        ]
+
     return pl.pallas_call(
         functools.partial(kernel, nrow, ncol),
         out_shape=jax.ShapeDtypeStruct((seq, cols), jnp.bfloat16),
-        in_specs=[vmem] * 5 + [pl.BlockSpec(memory_space=pl.ANY)],
+        in_specs=[pl.BlockSpec(memory_space=pltpu.HBM)] * 6,
         out_specs=vmem,
         scratch_shapes=[
+            *[pltpu.VMEM((seq, width), jnp.bfloat16)] * 4,
+            pltpu.VMEM((1, width), jnp.float32),
             pltpu.VMEM((depth, cols), jnp.bfloat16),
             pltpu.VMEM((seq, width), jnp.float32),
             pltpu.VMEM((ncol, 8, seq), jnp.float32),
             pltpu.VMEM((CHUNKS, nz, ct, width), jnp.bfloat16),
             pltpu.VMEM((CHUNKS, ratio, nrow, ct, width), jnp.bfloat16),
-            pltpu.VMEM((CHUNKS, nrow, ct, cols), jnp.bfloat16),
-            pltpu.VMEM((CHUNKS, nrow, ct, cols), jnp.bfloat16),
-            pltpu.VMEM((CHUNKS, ct, cols), jnp.float32),
-            pltpu.VMEM((nrow, ct, TILE), jnp.float32),
+            pltpu.VMEM((nrow, ct, tile), jnp.float32),
+            *sums(nlow, nhigh),
+            *sums(nhigh, nlow),
+            dma((5,)),
             dma,
             dma((ncol - 1,)),
             dma((ncol,)),
@@ -240,8 +345,14 @@
             dma((CHUNKS, per, nrow)),
             dma((CHUNKS, per)),
             dma((CHUNKS, per)),
-            dma((CHUNKS, nrow - 1)),
-            dma((CHUNKS, nrow)),
+            dma((CHUNKS, nlow)),
+            dma((CHUNKS, nlow)),
+            dma((CHUNKS, nhigh)),
+            dma((CHUNKS, nhigh)),
+            dma((CHUNKS, nhigh)),
+            dma((CHUNKS, nhigh)),
+            dma((CHUNKS, nlow)),
+            dma((CHUNKS, nlow)),
         ],
         compiler_params=pltpu.CompilerParams(
             collective_id=0, has_side_effects=True, vmem_limit_bytes=48 * 1024 * 1024

time: 70.9 us -> 64 us (0.903)
  Pallas kernels: 64.6 us -> 57.4 us
    pallas_call x1, Pallas kernels: 64.6 us -> 57.4 us  [per_device(): pl.pallas_call(functools.partial(kernel, nrow, ncol), out_shape=jax.Shape...]
where the time goes in v2:
time: 64 us; the launch traced here: 62.7 us
  Pallas kernels  57.4 us (90%)
  local copies, waits for them, and re-layouts  5.32 us (8%)
    pallas_call x1, Pallas kernels, per_device(): pl.pallas_call(functools.partial(kernel, nrow, ncol), out_shape=jax.Shape...  57.4 us
    unnamed x11, local copies, waits for them, and re-layouts  5.32 us

profile of v2, /device:TPU:0, one launch (start us, length us, event | category | flops | bytes accessed | tf_op | source)
XLA Modules:
  0.0 62.7 jit_solution(15254965093908982254)
XLA Ops:
  0.0 0.0 copy-start
  0.0 0.9 %copy-done = bf16[128,768]{1,0:T(8,128)(2,1)S(1)} copy-done((bf16[128,768]{1,0:T(8,128)(2,1)S(1)}, bf16[128,768]{1,0:T(8,128)(2,1)}, u32[]{:S(2)}) %copy-start) | copy-done | bytes 196632
  0.9 0.0 copy-start.1
  0.9 0.9 %copy-done.1 = bf16[128,768]{1,0:T(8,128)(2,1)S(1)} copy-done((bf16[128,768]{1,0:T(8,128)(2,1)S(1)}, bf16[128,768]{1,0:T(8,128)(2,1)}, u32[]{:S(2)}) %copy-start.1) | copy-done | bytes 196632
  1.9 0.0 copy-start.2
  1.9 0.9 %copy-done.2 = bf16[128,768]{1,0:T(8,128)(2,1)S(1)} copy-done((bf16[128,768]{1,0:T(8,128)(2,1)S(1)}, bf16[128,768]{1,0:T(8,128)(2,1)}, u32[]{:S(2)}) %copy-start.2) | copy-done | bytes 196632
  2.8 0.0 copy-start.3
  2.8 0.9 %copy-done.3 = bf16[128,768]{1,0:T(8,128)(2,1)S(1)} copy-done((bf16[128,768]{1,0:T(8,128)(2,1)S(1)}, bf16[128,768]{1,0:T(8,128)(2,1)}, u32[]{:S(2)}) %copy-start.3) | copy-done | bytes 196632
  3.7 0.0 copy-start.4
  3.7 0.7 %copy-done.4 = f32[6144]{0:T(1024)S(1)} copy-done((f32[6144]{0:T(1024)S(1)}, f32[6144]{0:T(1024)}, u32[]{:S(2)}) %copy-start.4) | copy-done | bytes 24600
  4.4 57.4 %shard_map.64 = bf16[128,3072]{1,0:T(8,128)(2,1)S(1)} custom-call(bf16[128,768]{1,0:T(8,128)(2,1)S(1)} %copy-done, bf16[128,768]{1,0:T(8,128)(2,1)S(1)} %copy-done.1, bf16[128,768]{1,0:T(8,128)(2,1)S(1)} %copy-done.2, bf16[128,768]{1,0:T(8,128)(2,1)S(1)} %copy-done.3, f32[1,6144]{1,0:T(1,128)S(1)} %bitcast.1, bf16[1536,3072]{1,0:T(8,128)(2,1)} %w_hbm.1), custom_call_target="tpu_custom_call" | custom-call | flops 4831838208 | bytes 11010048 | tf_op jit(solution)/shard_map/pallas_call | solution.py:322
  61.8 0.9 %copy.8 = bf16[128,3072]{1,0:T(8,128)(2,1)} copy(bf16[128,3072]{1,0:T(8,128)(2,1)S(1)} %shard_map.64) | data formatting | bytes 1572864
Async XLA Ops:
  0.0 0.9 %copy-start = (bf16[128,768]{1,0:T(8,128)(2,1)S(1)}, bf16[128,768]{1,0:T(8,128)(2,1)}, u32[]{:S(2)}) copy-start(bf16[128,768]{1,0:T(8,128)(2,1)} %q_hbm.1) | copy-start | bytes 589828
  0.9 0.9 %copy-start.1 = (bf16[128,768]{1,0:T(8,128)(2,1)S(1)}, bf16[128,768]{1,0:T(8,128)(2,1)}, u32[]{:S(2)}) copy-start(bf16[128,768]{1,0:T(8,128)(2,1)} %k_hbm.1) | copy-start | bytes 589828
  1.9 0.9 %copy-start.2 = (bf16[128,768]{1,0:T(8,128)(2,1)S(1)}, bf16[128,768]{1,0:T(8,128)(2,1)}, u32[]{:S(2)}) copy-start(bf16[128,768]{1,0:T(8,128)(2,1)} %v_hbm.1) | copy-start | bytes 589828
  2.8 0.9 %copy-start.3 = (bf16[128,768]{1,0:T(8,128)(2,1)S(1)}, bf16[128,768]{1,0:T(8,128)(2,1)}, u32[]{:S(2)}) copy-start(bf16[128,768]{1,0:T(8,128)(2,1)} %resid_hbm.1) | copy-start | bytes 589828
  3.7 0.7 %copy-start.4 = (f32[6144]{0:T(1024)S(1)}, f32[6144]{0:T(1024)}, u32[]{:S(2)}) copy-start(f32[6144]{0:T(1024)} %param.10) | copy-start | bytes 73732

commit v3 on v2

--- a/solution.py
+++ b/solution.py
@@ -10,7 +10,8 @@
 
 HD = 128
 CORES = 2
-CHUNKS = 4
+CHUNKS = 8
+GROUP = 3
 TILE = 512
 MESH = pl.DeviceIdType.MESH
 
@@ -28,15 +29,15 @@
 
 def kernel(
     nrow, ncol,
-    q_hbm, k_hbm, v_hbm, resid_hbm, gain_hbm, w_hbm, out_ref,
-    q_ref, k_ref, v_ref, resid_ref, gain_ref, w_ref, stream, stats, zbuf, xbuf, acc_ref,
+    q_hbm, k_hbm, v_hbm, resid_hbm, gain_hbm, w_hbm, out_hbm,
+    q_ref, k_ref, v_ref, resid_ref, gain_ref, w_ref, stream, stats, zbuf, xbuf, acc_ref, out_ref,
     one_p, one_r, one_own, two_p, two_r, two_own, other_one_p, other_one_r, other_one_own,
     other_two_p, other_two_r, other_two_own,
     in_sem, w_sem, st_s, st_r, z_s, z_r, p_s, p_r, b_s, b_r,
-    r1_s, r1_r, r2_s, r2_r, q1_s, q1_r, q2_s, q2_r,
+    out_sem, r1_s, r1_r, r2_s, r2_r, q1_s, q1_r, q2_s, q2_r,
 ):
     seq, width = q_ref.shape
-    cols = out_ref.shape[1]
+    cols = out_ref.shape[2]
     half = cols // 2
     tile = math.gcd(half, TILE)
     ratio = ncol // nrow
@@ -47,6 +48,7 @@
     z, core = lax.div(col, CORES), lax.rem(col, CORES)
     sibling = z * CORES + 1 - core
     sends = []
+    stores = []
 
     def remote(src, dst, send_sem, recv_sem, dev):
         return pltpu.make_async_remote_copy(
@@ -76,25 +78,38 @@
         load.wait()
 
     causal = lax.broadcasted_iota(jnp.int32, (seq, seq), 0) >= lax.broadcasted_iota(jnp.int32, (seq, seq), 1)
-    s1 = jnp.zeros((seq, 1), jnp.float32)
-    s2 = jnp.zeros((seq, 1), jnp.float32)
-    for h in range(width // HD):
-        cut = slice(h * HD, (h + 1) * HD)
-        scores = lax.dot_general(
-            q_ref[:, cut], k_ref[:, cut], (((1,), (1,)), ((), ())), preferred_element_type=jnp.float32
-        ) * (1.0 / math.sqrt(HD))
-        scores = jnp.where(causal, scores, -1e30)
-        expo = jnp.exp(scores - jnp.max(scores, axis=-1, keepdims=True))
-        prob = (expo / jnp.sum(expo, axis=-1, keepdims=True)).astype(jnp.bfloat16)
-        attended = jnp.dot(prob, v_ref[:, cut], preferred_element_type=jnp.float32).astype(jnp.bfloat16)
-        part = resid_ref[:, cut].astype(jnp.float32) + attended.astype(jnp.float32)
-        stream[:, cut] = part
-        s1 += jnp.sum(part, axis=1, keepdims=True)
-        s2 += jnp.sum(part * part, axis=1, keepdims=True)
-
-    lane = lax.broadcasted_iota(jnp.int32, (seq, HD), 1)
-    packed = jnp.where(lane == 0, s1, jnp.where(lane == 1, s2, 0.0))
-    stats[col] = packed.T[:8]
+    sum1 = jnp.zeros((seq, HD), jnp.float32)
+    sum2 = jnp.zeros((seq, HD), jnp.float32)
+    heads = width // HD
+    for first in range(0, heads, GROUP):
+        cuts = [slice(h * HD, (h + 1) * HD) for h in range(first, min(first + GROUP, heads))]
+        scores = [
+            lax.dot_general(
+                q_ref[:, cut], k_ref[:, cut], (((1,), (1,)), ((), ())), preferred_element_type=jnp.float32
+            ) * (1.0 / math.sqrt(HD))
+            for cut in cuts
+        ]
+        scores = [jnp.where(causal, x, -1e30) for x in scores]
+        highest = [jnp.max(x, axis=-1, keepdims=True) for x in scores]
+        expo = [jnp.exp(x - m) for x, m in zip(scores, highest)]
+        below = [jnp.sum(x, axis=-1, keepdims=True) for x in expo]
+        prob = [(x / m).astype(jnp.bfloat16) for x, m in zip(expo, below)]
+        attended = [
+            jnp.dot(x, v_ref[:, cut], preferred_element_type=jnp.float32).astype(jnp.bfloat16)
+            for x, cut in zip(prob, cuts)
+        ]
+        for x, cut in zip(attended, cuts):
+            part = resid_ref[:, cut].astype(jnp.float32) + x.astype(jnp.float32)
+            stream[:, cut] = part
+            sum1 += part
+            sum2 += part * part
+
+    place = lax.broadcasted_iota(jnp.int32, (8, seq), 0)
+    stats[col] = jnp.where(
+        place == 0,
+        jnp.sum(sum1.T, axis=0, keepdims=True),
+        jnp.where(place == 1, jnp.sum(sum2.T, axis=0, keepdims=True), 0.0),
+    )
     pl.semaphore_wait(barrier, ncol + nrow - 2)
     for d in range(1, ncol):
         copy = remote(stats.at[col], stats.at[col], st_s.at[d - 1], st_r.at[col], (row, lax.rem(col + d, ncol)))
@@ -275,7 +290,11 @@
                     u = u + way["r2"][s, lax.rem(two + e, way["n2"]), :, at].astype(jnp.float32)
                 u = 0.5 * u * (1.0 + jnp.tanh(math.sqrt(2.0 / math.pi) * (u + 0.044715 * (u * u * u))))
                 w_at = pl.ds(pl.multiple_of(way["start"] + n * tile, tile), tile)
-                out_ref[s * ct:(s + 1) * ct, w_at] = u.astype(jnp.bfloat16)
+                out_ref[s, :, w_at] = u.astype(jnp.bfloat16)
+
+        copy = pltpu.make_async_copy(out_ref.at[s], out_hbm.at[s * ct:(s + 1) * ct, :], out_sem.at[s])
+        copy.start()
+        stores.append(copy)
 
     to_rows(0)
     to_sibling(0)
@@ -294,6 +313,8 @@
         finish(s)
     for cond, copy in sends:
         guarded(cond, copy.wait_send)
+    for copy in stores:
+        copy.wait()
 
 
 def per_device(q_seq, k_seq, v_seq, resid, ln_gain, w_up):
@@ -303,7 +324,7 @@
     ratio, nz, ct = ncol // nrow, ncol // CORES, seq // CHUNKS
     per = max(1, ratio // CORES)
     dma = pltpu.SemaphoreType.DMA
-    vmem = pl.BlockSpec(memory_space=pltpu.VMEM)
+    hbm = pl.BlockSpec(memory_space=pltpu.HBM)
     half = cols // 2
     tile = math.gcd(half, TILE)
     nlow = low_count(nrow)
@@ -322,8 +343,8 @@
     return pl.pallas_call(
         functools.partial(kernel, nrow, ncol),
         out_shape=jax.ShapeDtypeStruct((seq, cols), jnp.bfloat16),
-        in_specs=[pl.BlockSpec(memory_space=pltpu.HBM)] * 6,
-        out_specs=vmem,
+        in_specs=[hbm] * 6,
+        out_specs=hbm,
         scratch_shapes=[
             *[pltpu.VMEM((seq, width), jnp.bfloat16)] * 4,
             pltpu.VMEM((1, width), jnp.float32),
@@ -333,6 +354,7 @@
             pltpu.VMEM((CHUNKS, nz, ct, width), jnp.bfloat16),
             pltpu.VMEM((CHUNKS, ratio, nrow, ct, width), jnp.bfloat16),
             pltpu.VMEM((nrow, ct, tile), jnp.float32),
+            pltpu.VMEM((CHUNKS, ct, cols), jnp.bfloat16),
             *sums(nlow, nhigh),
             *sums(nhigh, nlow),
             dma((5,)),
@@ -345,6 +367,7 @@
             dma((CHUNKS, per, nrow)),
             dma((CHUNKS, per)),
             dma((CHUNKS, per)),
+            dma((CHUNKS,)),
             dma((CHUNKS, nlow)),
             dma((CHUNKS, nlow)),
             dma((CHUNKS, nhigh)),
@@ -355,7 +378,7 @@
             dma((CHUNKS, nlow)),
         ],
         compiler_params=pltpu.CompilerParams(
-            collective_id=0, has_side_effects=True, vmem_limit_bytes=48 * 1024 * 1024
+            collective_id=0, has_side_effects=True, vmem_limit_bytes=60 * 1024 * 1024
         ),
         cost_estimate=pl.CostEstimate(
             flops=2 * nrow * seq * depth * cols,

time: 64 us -> 68.7 us (1.073); the launches traced: 62.7 us -> 68.5 us
  Pallas kernels: 57.4 us -> 66.4 us
  local copies, waits for them, and re-layouts: 5.32 us -> 2.06 us
    pallas_call x1, Pallas kernels: 57.4 us -> 66.4 us  [per_device(): pl.pallas_call(functools.partial(kernel, nrow, ncol), out_shape=jax.Shape...]
    unnamed x11 -> x1, local copies, waits for them, and re-layouts: 5.32 us -> 2.06 us
where the time goes in v3:
time: 68.7 us; the launch traced here: 68.5 us
  Pallas kernels  66.4 us (97%)
  local copies, waits for them, and re-layouts  2.06 us (3%)
    pallas_call x1, Pallas kernels, per_device(): pl.pallas_call(functools.partial(kernel, nrow, ncol), out_shape=jax.Shape...  66.4 us
    unnamed x1, local copies, waits for them, and re-layouts  2.06 us

profile of v3, /device:TPU:0, one launch (start us, length us, event | category | flops | bytes accessed | tf_op | source)
XLA Modules:
  0.0 68.5 jit_solution(17725021046256523589)
XLA Ops:
  0.0 66.4 %shard_map.64 = bf16[128,3072]{1,0:T(8,128)(2,1)} custom-call(bf16[128,768]{1,0:T(8,128)(2,1)} %q_hbm.1, bf16[128,768]{1,0:T(8,128)(2,1)} %k_hbm.1, bf16[128,768]{1,0:T(8,128)(2,1)} %v_hbm.1, bf16[128,768]{1,0:T(8,128)(2,1)} %resid_hbm.1, f32[1,6144]{1,0:T(1,128)} %bitcast.1, bf16[1536,3072]{1,0:T(8,128)(2,1)} %w_hbm.1), custom_call_target="tpu_custom_call" | custom-call | flops 4831838208 | bytes 11010048 | tf_op jit(solution)/shard_map/pallas_call | solution.py:343
  66.4 2.1 %copy.8 = bf16[128,3072]{1,0:T(8,128)(2,1)} copy(bf16[128,3072]{1,0:T(8,128)(2,1)} %shard_map.64) | data formatting | bytes 1572864

commit v4 on v3

v4 whole, which is shorter than its diff:
```python
import functools
import math

import jax
import jax.numpy as jnp
from jax import lax
from jax.experimental import pallas as pl
from jax.experimental.pallas import tpu as pltpu
from jax.sharding import PartitionSpec as P

HD = 128
CORES = 2
CHUNKS = 4
SPANS = ((0, 1), (1, 2), (2, 4))
GROUP = 3
TILE = 512
MESH = pl.DeviceIdType.MESH


def guarded(cond, fn):
    if cond is True:
        fn()
    else:
        pl.when(cond)(fn)


def low_count(nrow):
    return max(n for n in range(1, math.isqrt(nrow) + 1) if nrow % n == 0)


def kernel(
    nrow, ncol,
    q_hbm, k_hbm, v_hbm, resid_hbm, gain_hbm, w_hbm, out_ref,
    q_ref, k_ref, v_ref, resid_ref, gain_ref, w_ref, stream, stats, zbuf, xbuf, acc_ref,
    one_p, one_r, one_own, two_p, two_r, two_own, other_one_p, other_one_r, other_one_own,
    other_two_p, other_two_r, other_two_own,
    in_sem, w_sem, st_s, st_r, z_s, z_r, p_s, p_r, b_s, b_r,
    r1_s, r1_r, r2_s, r2_r, q1_s, q1_r, q2_s, q2_r,
):
    seq, width = q_ref.shape
    cols = out_ref.shape[1]
    half = cols // 2
    tile = math.gcd(half, TILE)
    ratio = ncol // nrow
    nz = ncol // CORES
    ct = seq // CHUNKS
    full = width * ncol
    row, col = lax.axis_index("row"), lax.axis_index("col")
    z, core = lax.div(col, CORES), lax.rem(col, CORES)
    sibling = z * CORES + 1 - core
    sends = []

    def remote(src, dst, send_sem, recv_sem, dev):
        return pltpu.make_async_remote_copy(
            src_ref=src, dst_ref=dst, send_sem=send_sem, recv_sem=recv_sem,
            device_id=dev, device_id_type=MESH,
        )

    loads = [
        pltpu.make_async_copy(src, dst, in_sem.at[i])
        for i, (src, dst) in enumerate((
            (q_hbm, q_ref), (k_hbm, k_ref), (v_hbm, v_ref), (resid_hbm, resid_ref),
            (gain_hbm.at[:, pl.ds(pl.multiple_of(col * width, 128), width)], gain_ref),
        ))
    ]
    w_copy = pltpu.make_async_copy(w_hbm, w_ref, w_sem)
    for load in loads:
        load.start()
    w_copy.start()

    barrier = pltpu.get_barrier_semaphore()
    for d in range(1, ncol):
        pl.semaphore_signal(barrier, inc=1, device_id=(row, lax.rem(col + d, ncol)), device_id_type=MESH)
    for d in range(1, nrow):
        pl.semaphore_signal(barrier, inc=1, device_id=(lax.rem(row + d, nrow), col), device_id_type=MESH)

    for load in loads:
        load.wait()

    causal = lax.broadcasted_iota(jnp.int32, (seq, seq), 0) >= lax.broadcasted_iota(jnp.int32, (seq, seq), 1)
    sum1 = jnp.zeros((seq, HD), jnp.float32)
    sum2 = jnp.zeros((seq, HD), jnp.float32)
    heads = width // HD
    for first in range(0, heads, GROUP):
        cuts = [slice(h * HD, (h + 1) * HD) for h in range(first, min(first + GROUP, heads))]
        scores = [
            lax.dot_general(
                q_ref[:, cut], k_ref[:, cut], (((1,), (1,)), ((), ())), preferred_element_type=jnp.float32
            ) * (1.0 / math.sqrt(HD))
            for cut in cuts
        ]
        scores = [jnp.where(causal, x, -1e30) for x in scores]
        highest = [jnp.max(x, axis=-1, keepdims=True) for x in scores]
        expo = [jnp.exp(x - m) for x, m in zip(scores, highest)]
        below = [jnp.sum(x, axis=-1, keepdims=True) for x in expo]
        prob = [(x / m).astype(jnp.bfloat16) for x, m in zip(expo, below)]
        attended = [
            jnp.dot(x, v_ref[:, cut], preferred_element_type=jnp.float32).astype(jnp.bfloat16)
            for x, cut in zip(prob, cuts)
        ]
        for x, cut in zip(attended, cuts):
            part = resid_ref[:, cut].astype(jnp.float32) + x.astype(jnp.float32)
            stream[:, cut] = part
            sum1 += part
            sum2 += part * part

    place = lax.broadcasted_iota(jnp.int32, (8, seq), 0)
    stats[col] = jnp.where(
        place == 0,
        jnp.sum(sum1.T, axis=0, keepdims=True),
        jnp.where(place == 1, jnp.sum(sum2.T, axis=0, keepdims=True), 0.0),
    )
    pl.semaphore_wait(barrier, ncol + nrow - 2)
    for d in range(1, ncol):
        copy = remote(stats.at[col], stats.at[col], st_s.at[d - 1], st_r.at[col], (row, lax.rem(col + d, ncol)))
        copy.start()
        sends.append((True, copy))
    for d in range(1, ncol):
        other = lax.rem(col + d, ncol)
        remote(stats.at[other], stats.at[other], st_s.at[d - 1], st_r.at[other], (row, other)).wait_recv()
    total = stats[0]
    for c in range(1, ncol):
        total += stats[c]
    spread_out = jnp.concatenate([total] * (seq // 8), axis=0).T
    mean = spread_out[:, 0:1] / full
    spread = spread_out[:, 1:2] / full - mean * mean
    inv = lax.rsqrt(spread + 1e-05)
    gain = gain_ref[...]

    def along_z(s):
        copies = []
        for d in range(1, nz):
            dev = (row, lax.rem(z + d, nz) * CORES + core)
            copy = remote(zbuf.at[s, z], zbuf.at[s, z], z_s.at[s, d - 1], z_r.at[s, z], dev)
            copy.start()
            copies.append(copy)
        return copies

    def normalize(s):
        rows = slice(s * ct, (s + 1) * ct)
        zbuf[s, z] = ((stream[rows, :] - mean[rows]) * inv[rows] * gain).astype(jnp.bfloat16)

    normalize(0)
    leaving = [along_z(0)]
    for s in range(1, CHUNKS):
        normalize(s)

    if ratio % CORES == 0:
        mine = [CORES * i + core for i in range(ratio // CORES)]
        theirs = [CORES * i + 1 - core for i in range(ratio // CORES)]
        holds = lambda r: True
        lacks = lambda r: True
    else:
        mine, theirs = [0], [0]
        holds = lambda r: lax.rem(r, CORES) == core
        lacks = lambda r: lax.rem(r, CORES) != core

    nlow = low_count(nrow)
    nhigh = nrow // nlow
    high, low_at = lax.div(row, nlow), lax.rem(row, nlow)
    ways = [
        dict(
            start=0, n1=nlow, n2=nhigh, one=low_at, two=high, index=lambda i, m: m * nlow + i,
            p1=one_p, r1=one_r, own1=one_own, p2=two_p, r2=two_r, own2=two_own,
            s1_s=r1_s, s1_r=r1_r, s2_s=r2_s, s2_r=r2_r,
        ),
        dict(
            start=half, n1=nhigh, n2=nlow, one=high, two=low_at, index=lambda i, m: i * nlow + m,
            p1=other_one_p, r1=other_one_r, own1=other_one_own, p2=other_two_p, r2=other_two_r,
            own2=other_two_own, s1_s=q1_s, s1_r=q1_r, s2_s=q2_s, s2_r=q2_r,
        ),
    ]

    def to_rows(s):
        for copy in leaving[s]:
            copy.wait_send()
        if s + 1 < CHUNKS:
            leaving.append(along_z(s + 1))
        for d in range(1, nz):
            other = lax.rem(z + d, nz)
            remote(
                zbuf.at[s, other], zbuf.at[s, other], z_s.at[s, d - 1], z_r.at[s, other],
                (row, other * CORES + core),
            ).wait_recv()
        for i, j in enumerate(mine):
            for d in range(1, nrow):
                to = lax.rem(row + d, nrow)
                copy = remote(
                    zbuf.at[s, lax.div(to * ratio + j, CORES)], xbuf.at[j, s, row],
                    p_s.at[s, i, d - 1], p_r.at[s, i, row], (to, col),
                )
                guarded(holds(to), copy.start)
                sends.append((holds(to), copy))

            def keep(j=j):
                xbuf[j, s, row] = zbuf[s, lax.div(row * ratio + j, CORES)]

            guarded(holds(row), keep)

    def to_sibling(s):
        for i, j in enumerate(mine):

            def pass_on(i=i, j=j):
                for d in range(1, nrow):
                    src = lax.rem(row + d, nrow)
                    remote(
                        xbuf.at[j, s, src], xbuf.at[j, s, src], p_s.at[s, i, d - 1], p_r.at[s, i, src],
                        (src, col),
                    ).wait_recv()
                remote(xbuf.at[j, s], xbuf.at[j, s], b_s.at[s, i], b_r.at[s, i], (row, sibling)).start()

            guarded(holds(row), pass_on)
            sends.append((
                holds(row),
                remote(xbuf.at[j, s], xbuf.at[j, s], b_s.at[s, i], b_r.at[s, i], (row, sibling)),
            ))

    def from_sibling(s):
        for i, j in enumerate(theirs):
            copy = remote(xbuf.at[j, s], xbuf.at[j, s], b_s.at[s, i], b_r.at[s, i], (row, sibling))
            guarded(lacks(row), copy.wait_recv)

    def multiply(g, n, way):
        u0, u1 = SPANS[g]
        one, two, n1, n2, index = way["one"], way["two"], way["n1"], way["n2"], way["index"]
        w_at = slice(way["start"] + n * tile, way["start"] + (n + 1) * tile)
        acc = None
        for j in range(ratio):
            term = jnp.dot(
                xbuf[j, u0:u1].reshape((u1 - u0) * nrow * ct, width), w_ref[j * width:(j + 1) * width, w_at],
                preferred_element_type=jnp.float32,
            )
            acc = term if acc is None else acc + term
        acc = acc.reshape(u1 - u0, nrow, ct, tile)
        acc_ref[:u1 - u0] = acc
        low = acc.astype(jnp.bfloat16)
        for i in range(n1):
            for m in range(n2):
                way["p1"][n, i, u0:u1, m] = low[:, index(i, m)]
        for d in range(1, n1):
            to = lax.rem(one + d, n1)
            copy = remote(
                way["p1"].at[n, to, u0:u1], way["r1"].at[n, one, u0:u1],
                way["s1_s"].at[g, n, d - 1], way["s1_r"].at[g, n, one], (index(to, two), col),
            )
            copy.start()
            sends.append((True, copy))
        for m in range(n2):
            way["own1"][n, u0:u1, m] = acc_ref[:u1 - u0, index(one, m)]

    def add_first(g, n, way):
        u0, u1 = SPANS[g]
        one, two, n1, n2, index = way["one"], way["two"], way["n1"], way["n2"], way["index"]
        for d in range(1, n1):
            src = lax.rem(one + d, n1)
            remote(
                way["p1"].at[n, src, u0:u1], way["r1"].at[n, src, u0:u1],
                way["s1_s"].at[g, n, d - 1], way["s1_r"].at[g, n, src], (index(src, two), col),
            ).wait_recv()
        for e in list(range(1, n2)) + [0]:
            to = lax.rem(two + e, n2)
            u = way["own1"][n, u0:u1, to]
            for d in range(1, n1):
                u = u + way["r1"][n, lax.rem(one + d, n1), u0:u1, to].astype(jnp.float32)
            if e:
                way["p2"][n, to, u0:u1] = u.astype(jnp.bfloat16)
                copy = remote(
                    way["p2"].at[n, to, u0:u1], way["r2"].at[n, two, u0:u1],
                    way["s2_s"].at[g, n, e - 1], way["s2_r"].at[g, n, two], (index(one, to), col),
                )
                copy.start()
                sends.append((True, copy))
            else:
                way["own2"][n, u0:u1] = u

    def finish(g, n, way):
        u0, u1 = SPANS[g]
        one, two, n2, index = way["one"], way["two"], way["n2"], way["index"]
        for e in range(1, n2):
            src = lax.rem(two + e, n2)
            remote(
                way["p2"].at[n, src, u0:u1], way["r2"].at[n, src, u0:u1],
                way["s2_s"].at[g, n, e - 1], way["s2_r"].at[g, n, src], (index(one, src), col),
            ).wait_recv()
        u = way["own2"][n, u0:u1]
        for e in range(1, n2):
            u = u + way["r2"][n, lax.rem(two + e, n2), u0:u1].astype(jnp.float32)
        u = 0.5 * u * (1.0 + jnp.tanh(math.sqrt(2.0 / math.pi) * (u + 0.044715 * (u * u * u))))
        w_at = slice(way["start"] + n * tile, way["start"] + (n + 1) * tile)
        out_ref[u0 * ct:u1 * ct, w_at] = u.astype(jnp.bfloat16).reshape((u1 - u0) * ct, tile)

    pieces = [(n, way) for n in range(half // tile) for way in ways]

    def each(fn, g):
        for n, way in pieces:
            fn(g, n, way)

    to_rows(0)
    to_sibling(0)
    last = len(SPANS) - 1
    for g, (u0, u1) in enumerate(SPANS):
        for s in range(u0, u1):
            from_sibling(s)
        if g == 0:
            w_copy.wait()
        if u1 < CHUNKS:
            to_rows(u1)
        each(multiply, g)
        if g < last:
            to_sibling(u1)
            for s in range(u1 + 1, SPANS[g + 1][1]):
                to_rows(s)
                to_sibling(s)
        if g:
            each(add_first, g - 1)
    for g in range(last - 1):
        each(finish, g)
    for i, (n, way) in enumerate(pieces):
        add_first(last, n, way)
        finish(last - 1, n, way)
    each(finish, last)
    for cond, copy in sends:
        guarded(cond, copy.wait_send)


def per_device(q_seq, k_seq, v_seq, resid, ln_gain, w_up):
    nrow, ncol = lax.axis_size("row"), lax.axis_size("col")
    seq, width = q_seq.shape
    depth, cols = w_up.shape
    ratio, nz, ct = ncol // nrow, ncol // CORES, seq // CHUNKS
    per = max(1, ratio // CORES)
    dma = pltpu.SemaphoreType.DMA
    hbm = pl.BlockSpec(memory_space=pltpu.HBM)
    half = cols // 2
    tile = math.gcd(half, TILE)
    nlow = low_count(nrow)
    nhigh = nrow // nlow

    count = half // tile
    span = max(u1 - u0 for u0, u1 in SPANS)

    def sums(n1, n2):
        return [
            pltpu.VMEM((count, n1, CHUNKS, n2, ct, tile), jnp.bfloat16),
            pltpu.VMEM((count, n1, CHUNKS, n2, ct, tile), jnp.bfloat16),
            pltpu.VMEM((count, CHUNKS, n2, ct, tile), jnp.float32),
            pltpu.VMEM((count, n2, CHUNKS, ct, tile), jnp.bfloat16),
            pltpu.VMEM((count, n2, CHUNKS, ct, tile), jnp.bfloat16),
            pltpu.VMEM((count, CHUNKS, ct, tile), jnp.float32),
        ]

    return pl.pallas_call(
        functools.partial(kernel, nrow, ncol),
        out_shape=jax.ShapeDtypeStruct((seq, cols), jnp.bfloat16),
        in_specs=[hbm] * 6,
        out_specs=pl.BlockSpec(memory_space=pltpu.VMEM),
        scratch_shapes=[
            *[pltpu.VMEM((seq, width), jnp.bfloat16)] * 4,
            pltpu.VMEM((1, width), jnp.float32),
            pltpu.VMEM((depth, cols), jnp.bfloat16),
            pltpu.VMEM((seq, width), jnp.float32),
            pltpu.VMEM((ncol, 8, seq), jnp.float32),
            pltpu.VMEM((CHUNKS, nz, ct, width), jnp.bfloat16),
            pltpu.VMEM((ratio, CHUNKS, nrow, ct, width), jnp.bfloat16),
            pltpu.VMEM((span, nrow, ct, tile), jnp.float32),
            *sums(nlow, nhigh),
            *sums(nhigh, nlow),
            dma((5,)),
            dma,
            dma((ncol - 1,)),
            dma((ncol,)),
            dma((CHUNKS, nz - 1)),
            dma((CHUNKS, nz)),
            dma((CHUNKS, per, nrow - 1)),
            dma((CHUNKS, per, nrow)),
            dma((CHUNKS, per)),
            dma((CHUNKS, per)),
            dma((len(SPANS), count, nlow)),
            dma((len(SPANS), count, nlow)),
            dma((len(SPANS), count, nhigh)),
            dma((len(SPANS), count, nhigh)),
            dma((len(SPANS), count, nhigh)),
            dma((len(SPANS), count, nhigh)),
            dma((len(SPANS), count, nlow)),
            dma((len(SPANS), count, nlow)),
        ],
        compiler_params=pltpu.CompilerParams(
            collective_id=0, has_side_effects=True, vmem_limit_bytes=60 * 1024 * 1024
        ),
        cost_estimate=pl.CostEstimate(
            flops=2 * nrow * seq * depth * cols,
            bytes_accessed=2 * (depth * cols + seq * cols + 4 * seq * width),
            transcendentals=seq * cols,
        ),
    )(q_seq, k_seq, v_seq, resid, ln_gain.reshape(1, -1), w_up)


def solution(mesh):
    placed = (
        P("row", "col"),
        P("row", "col"),
        P("row", "col"),
        P("row", "col"),
        P(),
        P("row", "col"),
    )
    return jax.shard_map(
        per_device, mesh=mesh, in_specs=placed, out_specs=P("row", "col"), check_vma=False
    )
```

time: 68.7 us -> 64.7 us (0.942)
  Pallas kernels: 66.4 us -> 62.2 us
    pallas_call x1, Pallas kernels: 66.4 us -> 62.2 us  [per_device(): pl.pallas_call(functools.partial(kernel, nrow, ncol), out_shape=jax.Shape...]
where the time goes in v4:
time: 64.7 us; the launch traced here: 64.3 us
  Pallas kernels  62.2 us (96%)
  local copies, waits for them, and re-layouts  2.06 us (3%)
    pallas_call x1, Pallas kernels, per_device(): pl.pallas_call(functools.partial(kernel, nrow, ncol), out_shape=jax.Shape...  62.2 us
    unnamed x1, local copies, waits for them, and re-layouts  2.06 us

profile of v4, /device:TPU:0, one launch (start us, length us, event | category | flops | bytes accessed | tf_op | source)
XLA Modules:
  0.0 64.3 jit_solution(14348937313059531389)
XLA Ops:
  0.0 62.2 %shard_map.64 = bf16[128,3072]{1,0:T(8,128)(2,1)} custom-call(bf16[128,768]{1,0:T(8,128)(2,1)} %q_hbm.1, bf16[128,768]{1,0:T(8,128)(2,1)} %k_hbm.1, bf16[128,768]{1,0:T(8,128)(2,1)} %v_hbm.1, bf16[128,768]{1,0:T(8,128)(2,1)} %resid_hbm.1, f32[1,6144]{1,0:T(1,128)} %bitcast.1, bf16[1536,3072]{1,0:T(8,128)(2,1)} %w_hbm.1), custom_call_target="tpu_custom_call" | custom-call | flops 4831838208 | bytes 11010048 | tf_op jit(solution)/shard_map/pallas_call | solution.py:352
  62.2 2.1 %copy.8 = bf16[128,3072]{1,0:T(8,128)(2,1)} copy(bf16[128,3072]{1,0:T(8,128)(2,1)} %shard_map.64) | data formatting | bytes 1572864

commit v5 on v4

--- a/solution.py
+++ b/solution.py
@@ -66,7 +66,6 @@
     w_copy = pltpu.make_async_copy(w_hbm, w_ref, w_sem)
     for load in loads:
         load.start()
-    w_copy.start()
 
     barrier = pltpu.get_barrier_semaphore()
     for d in range(1, ncol):
@@ -76,6 +75,7 @@
 
     for load in loads:
         load.wait()
+    w_copy.start()
 
     causal = lax.broadcasted_iota(jnp.int32, (seq, seq), 0) >= lax.broadcasted_iota(jnp.int32, (seq, seq), 1)
     sum1 = jnp.zeros((seq, HD), jnp.float32)
@@ -128,22 +128,19 @@
     gain = gain_ref[...]
 
     def along_z(s):
-        copies = []
         for d in range(1, nz):
             dev = (row, lax.rem(z + d, nz) * CORES + core)
             copy = remote(zbuf.at[s, z], zbuf.at[s, z], z_s.at[s, d - 1], z_r.at[s, z], dev)
             copy.start()
-            copies.append(copy)
-        return copies
+            sends.append((True, copy))
 
     def normalize(s):
         rows = slice(s * ct, (s + 1) * ct)
         zbuf[s, z] = ((stream[rows, :] - mean[rows]) * inv[rows] * gain).astype(jnp.bfloat16)
 
-    normalize(0)
-    leaving = [along_z(0)]
-    for s in range(1, CHUNKS):
+    for s in range(CHUNKS):
         normalize(s)
+        along_z(s)
 
     if ratio % CORES == 0:
         mine = [CORES * i + core for i in range(ratio // CORES)]
@@ -172,10 +169,6 @@
     ]
 
     def to_rows(s):
-        for copy in leaving[s]:
-            copy.wait_send()
-        if s + 1 < CHUNKS:
-            leaving.append(along_z(s + 1))
         for d in range(1, nz):
             other = lax.rem(z + d, nz)
             remote(
@@ -298,26 +291,28 @@
     to_rows(0)
     to_sibling(0)
     last = len(SPANS) - 1
+    ahead = 1
     for g, (u0, u1) in enumerate(SPANS):
+        if ahead < CHUNKS:
+            to_rows(ahead)
+            ahead += 1
+        if g > 1:
+            each(add_first, g - 2)
+        for s in range(max(u0, 1), u1):
+            to_sibling(s)
+            if s + 1 == u1 - 1 and g == last and g > 0:
+                each(add_first, g - 1)
+        if g == last and g > 0 and u1 - u0 == 1:
+            each(add_first, g - 1)
         for s in range(u0, u1):
             from_sibling(s)
         if g == 0:
             w_copy.wait()
-        if u1 < CHUNKS:
-            to_rows(u1)
         each(multiply, g)
-        if g < last:
-            to_sibling(u1)
-            for s in range(u1 + 1, SPANS[g + 1][1]):
-                to_rows(s)
-                to_sibling(s)
-        if g:
-            each(add_first, g - 1)
-    for g in range(last - 1):
+    for g in range(last):
         each(finish, g)
-    for i, (n, way) in enumerate(pieces):
+    for n, way in pieces:
         add_first(last, n, way)
-        finish(last - 1, n, way)
     each(finish, last)
     for cond, copy in sends:
         guarded(cond, copy.wait_send)

time: 64.7 us -> 60.4 us (0.934); the launches traced: 64.3 us -> 59.2 us
  Pallas kernels: 62.2 us -> 57.2 us
    pallas_call x1, Pallas kernels: 62.2 us -> 57.2 us  [per_device(): pl.pallas_call(functools.partial(kernel, nrow, ncol), out_shape=jax.Shape...]
where the time goes in v5:
time: 60.4 us; the launch traced here: 59.2 us
  Pallas kernels  57.2 us (95%)
  local copies, waits for them, and re-layouts  2.06 us (3%)
    pallas_call x1, Pallas kernels, per_device(): pl.pallas_call(functools.partial(kernel, nrow, ncol), out_shape=jax.Shape...  57.2 us
    unnamed x1, local copies, waits for them, and re-layouts  2.06 us

profile of v5, /device:TPU:0, one launch (start us, length us, event | category | flops | bytes accessed | tf_op | source)
XLA Modules:
  0.0 59.2 jit_solution(9942437755737743939)
XLA Ops:
  0.0 57.2 %shard_map.64 = bf16[128,3072]{1,0:T(8,128)(2,1)} custom-call(bf16[128,768]{1,0:T(8,128)(2,1)} %q_hbm.1, bf16[128,768]{1,0:T(8,128)(2,1)} %k_hbm.1, bf16[128,768]{1,0:T(8,128)(2,1)} %v_hbm.1, bf16[128,768]{1,0:T(8,128)(2,1)} %resid_hbm.1, f32[1,6144]{1,0:T(1,128)} %bitcast.1, bf16[1536,3072]{1,0:T(8,128)(2,1)} %w_hbm.1), custom_call_target="tpu_custom_call" | custom-call | flops 4831838208 | bytes 11010048 | tf_op jit(solution)/shard_map/pallas_call | solution.py:347
  57.2 2.1 %copy.8 = bf16[128,3072]{1,0:T(8,128)(2,1)} copy(bf16[128,3072]{1,0:T(8,128)(2,1)} %shard_map.64) | data formatting | bytes 1572864

commit v6 on v5

--- a/solution.py
+++ b/solution.py
@@ -11,7 +11,7 @@
 HD = 128
 CORES = 2
 CHUNKS = 4
-SPANS = ((0, 1), (1, 2), (2, 4))
+SPANS = ((0, 1), (1, 2), (2, 3), (3, 4))
 GROUP = 3
 TILE = 512
 MESH = pl.DeviceIdType.MESH

time: 60.4 us -> 61 us (level)
  Pallas kernels: 57.2 us -> 58 us
    pallas_call x1, Pallas kernels: 57.2 us -> 58 us  [per_device(): pl.pallas_call(functools.partial(kernel, nrow, ncol), out_shape=jax.Shape...]
where the time goes in v6:
time: 61 us; the launch traced here: 60.1 us
  Pallas kernels  58 us (95%)
  local copies, waits for them, and re-layouts  2.06 us (3%)
    pallas_call x1, Pallas kernels, per_device(): pl.pallas_call(functools.partial(kernel, nrow, ncol), out_shape=jax.Shape...  58 us
    unnamed x1, local copies, waits for them, and re-layouts  2.06 us

profile of v6, /device:TPU:0, one launch (start us, length us, event | category | flops | bytes accessed | tf_op | source)
XLA Modules:
  0.0 60.1 jit_solution(8509693395298579408)
XLA Ops:
  0.0 58.0 %shard_map.64 = bf16[128,3072]{1,0:T(8,128)(2,1)} custom-call(bf16[128,768]{1,0:T(8,128)(2,1)} %q_hbm.1, bf16[128,768]{1,0:T(8,128)(2,1)} %k_hbm.1, bf16[128,768]{1,0:T(8,128)(2,1)} %v_hbm.1, bf16[128,768]{1,0:T(8,128)(2,1)} %resid_hbm.1, f32[1,6144]{1,0:T(1,128)} %bitcast.1, bf16[1536,3072]{1,0:T(8,128)(2,1)} %w_hbm.1), custom_call_target="tpu_custom_call" | custom-call | flops 4831838208 | bytes 11010048 | tf_op jit(solution)/shard_map/pallas_call | solution.py:347
  58.0 2.1 %copy.8 = bf16[128,3072]{1,0:T(8,128)(2,1)} copy(bf16[128,3072]{1,0:T(8,128)(2,1)} %shard_map.64) | data formatting | bytes 1572864
